TPU v7x, 32 devices: a whole 2x2x4 slice. The times are simulated.
32 devices in a mesh: ctx: 16 (over z, y, core), ch: 2 (over x).
Axes of the slice: x: 2, y: 2, z: 4, core: 2. Of those that a mesh axis runs over, the one named last changes fastest.
Arguments:
- grad_out: bfloat16 [2, 32, 65536], P(None, 'ch', 'ctx'), may hold values from -6 to 6
- inputs: bfloat16 [2, 32, 65536], P(None, 'ch', 'ctx'), may hold values from -6 to 6
- gates: bfloat16 [2, 32, 65536], P(None, 'ch', 'ctx'), may hold values from -6 to 6
- residues: float32 [512], P(('ctx', 'ch')), may hold values from -1.5 to 1.5
- rates: float32 [512], P(('ctx', 'ch')), as said below
- skip: float32 [32], P('ch'), may hold values from 0.5 to 1.5
Outputs:
- d_input: bfloat16 [2, 32, 65536], P(None, 'ch', 'ctx')
- d_gate: bfloat16 [2, 32, 65536], P(None, 'ch', 'ctx')
- d_residues: float32 [512], P(('ctx', 'ch'))
- d_log_rates: float32 [512], P(('ctx', 'ch'))
- d_skip: float32 [32], P('ch')
Inputs may be any that keep to these rules, and one draw needn't show every extreme that they name: `rates`: every rate is positive and at most 1 / 40.
All inputs are finite; a program needn't handle non-finite values.
Results may differ from a plain program's by a relative error of at most 0.01.
Values may be sent and summed in bfloat16 or wider, within the bound.
A program may use at most 128 MiB of HBM per device.

v0:
```python
import functools

import jax
import jax.numpy as jnp
from jax import lax
from jax.experimental import pallas as pl
from jax.experimental.pallas import tpu as pltpu
from jax.sharding import PartitionSpec as P

ORDER = 16
CHUNK = 128
f32 = jnp.float32
bf16 = jnp.bfloat16
NT = (((1,), (1,)), ((), ()))
TN = (((0,), (0,)), ((), ()))
NN = (((1,), (0,)), ((), ()))


def dot(a, b, dims):
    return lax.dot_general(a, b, dims, preferred_element_type=f32)


def iota(shape, axis):
    return lax.broadcasted_iota(jnp.int32, shape, axis)


def turn(v, shift):
    shift = shift % CHUNK
    return v if shift == 0 else pltpu.roll(v, shift, axis=1)


def skew8(v, sign):
    row = iota((8, CHUNK), 0)
    for bit in (1, 2, 4):
        v = jnp.where((row // bit) % 2 == 1, turn(v, sign * bit), v)
    return v


def body(devs, grad_ref, input_ref, gate_ref, rcol_ref, gcol_ref, rlane_ref, skip_ref,
         din_ref, dgate_ref, out_ref,
         xs, gs, p0, p1, g0, g1, ys, zs, wl, send, slots, send_sem, recv_sem):
    seqs, chans, span = grad_ref.shape
    rows = seqs * chans
    count = span // CHUNK
    me = lax.axis_index("ctx")
    barrier = pltpu.get_barrier_semaphore()
    for d in range(1, devs):
        pl.semaphore_signal(barrier, inc=1, device_id={"ctx": lax.rem(me + d, devs)},
                            device_id_type=pl.DeviceIdType.MESH)

    lane = iota((ORDER, CHUNK), 1).astype(f32)
    rest = jnp.zeros((CHUNK - ORDER, CHUNK), bf16)

    for k in range(count):
        at = pl.ds(k * CHUNK, CHUNK)
        to = pl.ds(k * rows, rows)
        xs[to, :] = input_ref[:, :, at].astype(f32).reshape(rows, CHUNK)
        mid = grad_ref[:, :, at].astype(f32) * gate_ref[:, :, at].astype(f32)
        gs[to, :] = mid.astype(bf16).astype(f32).reshape(rows, CHUNK)

    def pick(c):
        return pl.ds(c, count * seqs, stride=chans)

    for c in range(chans):
        rc = rcol_ref[c * ORDER:(c + 1) * ORDER, :]
        x = xs[pick(c), :].astype(bf16)
        g = gs[pick(c), :].astype(bf16)
        dec = jnp.exp(-rc * lane)
        eg = jnp.exp(-rc * (lane + 1.0))
        ep = jnp.exp(-rc * (CHUNK - 1.0 - lane))
        wx = jnp.concatenate([ep.astype(bf16), rest, (ep * (CHUNK - 1.0 - lane)).astype(bf16), rest], 0)
        wg = jnp.concatenate([eg.astype(bf16), rest, (eg * (lane + 1.0)).astype(bf16), rest], 0)
        wd = jnp.concatenate([dec.astype(bf16), rest, (dec * lane).astype(bf16), rest], 0)
        px = dot(x, wx, NT)
        p0[pick(c), :] = px[:, :CHUNK]
        p1[pick(c), :] = px[:, CHUNK:]
        pg = dot(g, wg, NT)
        g0[pick(c), :] = pg[:, :CHUNK]
        g1[pick(c), :] = pg[:, CHUNK:]
        outer = dot(x, g, TN)
        acc = jnp.zeros((8, CHUNK), f32)
        for q in range(CHUNK // 8):
            piece = outer[8 * q:8 * q + 8]
            keep = iota((8, CHUNK), 1) >= iota((8, CHUNK), 0) + 8 * q
            acc = acc + turn(jnp.where(keep, piece, 0.0), -8 * q)
        acc = skew8(acc, -1)
        high = acc.astype(bf16)
        low = (acc - high.astype(f32)).astype(bf16)
        local = dot(high, wd, NT) + dot(low, wd, NT)
        local = jnp.sum(local, axis=0, keepdims=True)
        wl[0, c:c + 1, :] = local[:, :CHUNK]
        wl[1, c:c + 1, :] = local[:, CHUNK:]
        wl[2, c:c + 1, :] = jnp.sum(acc, axis=0, keepdims=True)

    rl = rlane_ref[...]
    fade = jnp.exp(-rl * CHUNK)
    zero = jnp.zeros((rows, CHUNK), f32)
    s0, s1, weighted, moment = zero, zero, zero, zero
    for k in range(count):
        to = pl.ds(k * rows, rows)
        a0, a1, b0, b1 = p0[to, :], p1[to, :], g0[to, :], g1[to, :]
        weighted = weighted + b0 * s0
        moment = moment + b1 * s0 + b0 * s1
        p0[to, :] = s0
        s0, s1 = fade * s0 + a0, fade * (s1 + CHUNK * s0) + a1
    r0, r1 = zero, zero
    for k in reversed(range(count)):
        to = pl.ds(k * rows, rows)
        b0, b1 = g0[to, :], g1[to, :]
        g0[to, :] = r0
        r0, r1 = fade * r0 + b0, fade * (r1 + CHUNK * r0) + b1

    def pack(v):
        total = v[0:8]
        for q in range(1, rows // 8):
            total = total + turn(v[8 * q:8 * q + 8], ORDER * q)
        return total

    def unpack(v):
        keep = iota((8, CHUNK), 1) < ORDER
        return jnp.concatenate([jnp.where(keep, turn(v, -ORDER * q), 0.0) for q in range(rows // 8)], 0)

    send[0] = pack(s0)
    send[1] = pack(r0)
    pl.semaphore_wait(barrier, devs - 1)
    copies = []
    for d in range(1, devs):
        copy = pltpu.make_async_remote_copy(
            src_ref=send.at[(me + d) // devs],
            dst_ref=slots.at[me],
            send_sem=send_sem.at[d],
            recv_sem=recv_sem.at[d],
            device_id={"ctx": lax.rem(me + d, devs)},
            device_id_type=pl.DeviceIdType.MESH,
        )
        copy.start()
        copies.append(copy)

    for c in range(chans):
        rc = rcol_ref[c * ORDER:(c + 1) * ORDER, :]
        gc = gcol_ref[c * ORDER:(c + 1) * ORDER, :]
        kern = jnp.sum(gc * jnp.exp(-rc * lane), axis=0, keepdims=True)
        base = skew8(jnp.broadcast_to(kern, (8, CHUNK)), 1)
        parts = []
        for q in range(CHUNK // 8):
            keep = iota((8, CHUNK), 1) >= iota((8, CHUNK), 0) + 8 * q
            parts.append(jnp.where(keep, turn(base, 8 * q), 0.0))
        toep = jnp.concatenate(parts, 0).astype(bf16)
        x = xs[pick(c), :]
        g = gs[pick(c), :]
        sk = skip_ref[c:c + 1, :]
        ys[pick(c), :] = dot(x.astype(bf16), toep, NN) + sk * x
        zs[pick(c), :] = dot(g.astype(bf16), toep, NT) + sk * g

    for copy in copies:
        copy.wait()
    rp = pack(rl)
    s_in, sn_in, r_in = (jnp.zeros((8, CHUNK), f32) for _ in range(3))
    for d in range(1, devs):
        v = slots[lax.rem(me + devs - d, devs)]
        left = jnp.where(me >= d, 1.0, 0.0)
        term = left * jnp.exp(-rp * (span * (d - 1.0))) * v
        s_in = s_in + term
        sn_in = sn_in + (span * (d - 1.0)) * term
        r_in = r_in + (1.0 - left) * jnp.exp(-rp * (span * (devs - d - 1.0))) * v
    s_in, sn_in, r_in = unpack(s_in), unpack(sn_in), unpack(r_in)
    weighted = weighted + r0 * s_in
    moment = moment + r1 * s_in + r0 * sn_in + s1 * r_in
    for s in range(seqs):
        wl[0] = wl[0] + weighted[s * chans:(s + 1) * chans]
        wl[1] = wl[1] + moment[s * chans:(s + 1) * chans]
    out_ref[...] = wl[...]

    for k in range(count):
        to = pl.ds(k * rows, rows)
        p0[to, :] = p0[to, :] + s_in
        s_in = s_in * fade
    for k in reversed(range(count)):
        to = pl.ds(k * rows, rows)
        g0[to, :] = g0[to, :] + r_in
        r_in = r_in * fade

    for c in range(chans):
        rc = rcol_ref[c * ORDER:(c + 1) * ORDER, :]
        gc = gcol_ref[c * ORDER:(c + 1) * ORDER, :]
        we = jnp.concatenate([(gc * jnp.exp(-rc * (lane + 1.0))).astype(bf16), rest], 0)
        wp = jnp.concatenate([(gc * jnp.exp(-rc * (CHUNK - 1.0 - lane))).astype(bf16), rest], 0)
        ys[pick(c), :] = ys[pick(c), :] + dot(p0[pick(c), :].astype(bf16), we, NN)
        zs[pick(c), :] = zs[pick(c), :] + dot(g0[pick(c), :].astype(bf16), wp, NN)

    for k in range(count):
        at = pl.ds(k * CHUNK, CHUNK)
        to = pl.ds(k * rows, rows)
        conv = ys[to, :].astype(bf16).astype(f32).reshape(seqs, chans, CHUNK)
        dgate_ref[:, :, at] = (grad_ref[:, :, at].astype(f32) * conv).astype(bf16)
        din_ref[:, :, at] = zs[to, :].astype(bf16).reshape(seqs, chans, CHUNK)


def shards(grad_out, inputs, gates, residues, rates, skip):
    seqs, chans, span = grad_out.shape
    devs = lax.axis_size("ctx")
    group = lax.axis_index("ch")
    tables = lax.all_gather(jnp.stack([residues, rates]), ("ctx", "ch"), axis=1, tiled=True)
    total = tables.shape[1] // ORDER
    tables = tables.reshape(2, total, ORDER)
    own = lax.dynamic_slice_in_dim(tables, group * chans, chans, axis=1)
    res, rate = own[0], own[1]
    amp = jnp.sqrt(2.0 * rate)
    wide = (chans * ORDER, CHUNK)
    rcol = jnp.broadcast_to(rate.reshape(-1, 1), wide)
    gcol = jnp.broadcast_to((res * amp).reshape(-1, 1), wide)
    rlane = jnp.pad(jnp.tile(rate, (seqs, 1)), ((0, 0), (0, CHUNK - ORDER)))
    skips = jnp.broadcast_to(skip[:, None], (chans, CHUNK))
    elems = span // CHUNK * seqs * chans
    big = pltpu.VMEM((elems, CHUNK), f32)
    vmem = pl.BlockSpec(memory_space=pltpu.VMEM)
    d_input, d_gate, sums = pl.pallas_call(
        functools.partial(body, devs),
        out_shape=(
            jax.ShapeDtypeStruct(grad_out.shape, bf16),
            jax.ShapeDtypeStruct(grad_out.shape, bf16),
            jax.ShapeDtypeStruct((3, chans, CHUNK), f32),
        ),
        in_specs=[vmem] * 7,
        out_specs=(vmem, vmem, vmem),
        scratch_shapes=[big] * 8 + [
            pltpu.VMEM((3, chans, CHUNK), f32),
            pltpu.VMEM((2, 8, CHUNK), f32),
            pltpu.VMEM((devs, 8, CHUNK), f32),
            pltpu.SemaphoreType.DMA((devs,)),
            pltpu.SemaphoreType.DMA((devs,)),
        ],
        compiler_params=pltpu.CompilerParams(
            collective_id=0, has_side_effects=True, vmem_limit_bytes=40 * 2 ** 20
        ),
    )(grad_out, inputs, gates, rcol, gcol, rlane, skips)
    factor = (seqs * span * devs) ** (-0.5)
    weighted, moment = sums[0, :, :ORDER], sums[1, :, :ORDER]
    d_res = factor * amp * weighted
    d_log = factor * res * amp * (0.5 * weighted - rate * moment)
    spread = jnp.zeros((2, total, ORDER), f32)
    spread = lax.dynamic_update_slice_in_dim(spread, jnp.stack([d_res, d_log]), group * chans, axis=1)
    spread = lax.psum_scatter(spread.reshape(2, -1), ("ctx", "ch"), scatter_dimension=1, tiled=True)
    d_skip = lax.psum(factor * sums[2, :, 0], "ctx")
    return (d_input, d_gate, spread[0], spread[1], d_skip)


def solution(mesh):
    wide = P(None, "ch", "ctx")
    flat = P(("ctx", "ch"))
    return jax.shard_map(
        shards,
        mesh=mesh,
        in_specs=(wide, wide, wide, flat, flat, P("ch")),
        out_specs=(wide, wide, flat, flat, P("ch")),
        check_vma=False,
    )
```

profile of v0, /device:TPU:0, one launch (start us, length us, event | category | flops | bytes accessed | tf_op | source)
XLA Modules:
  0.0 236.7 jit_solution(11195853446053641867)
XLA Ops:
  7.2 0.0 reduce-scatter.4.cloned.1.call-start
  7.2 0.0 copy-start.4
  7.2 0.0 copy-start.5
  7.2 0.6 copy-done.4
  7.9 0.0 copy-done.5
  7.9 69.7 %all-gather = f32[32,16,2]{1,2,0:T(2,128)S(1)} all-gather(f32[1,16,2]{1,2,0:T(2,128)S(1)} %maximum_bitcast_fusion), channel_id=1, replica_groups=mesh['ctx'=16,'ch'=2] {'ctx','ch'}, dimensions={0}, use_global_device_ids=true | all-gather | bytes 4224 | tf_op jit(solution)/shard_map/all_gather | solution.py:203
  77.6 0.0 copy-start
  77.6 0.0 copy-start.1
  77.6 0.1 reshape.39
  77.7 0.1 reshape.36
  77.8 0.1 broadcast_in_dim.10
  77.9 0.1 squeeze.6
  78.0 0.1 broadcast_in_dim.23.gcol_ref
  78.1 0.0 copy-start.3
  78.1 0.1 broadcast_in_dim.22.rcol_ref
  78.2 0.6 copy-done.3
  78.8 0.1 broadcast_in_dim.24.skip_ref
  78.8 0.0 copy-done
  78.8 0.0 copy-done.1
  78.8 0.0 copy-start.2
  78.8 1.0 copy-done.2
  79.8 11.3 %shard_map.101 = (bf16[2,16,4096]{2,1,0:T(8,128)(2,1)S(1)}, bf16[2,16,4096]{2,1,0:T(8,128)(2,1)S(1)}, f32[3,16,128]{2,1,0:T(8,128)S(1)}) custom-call(bf16[2,16,4096]{2,1,0:T(8,128)(2,1)S(1)} %copy-done, bf16[2,16,4096]{2,1,0:T(8,128)(2,1)S(1)} %copy-done.1, bf16[2,16,4096]{2,1,0:T(8,128)(2,1)S(1)} %copy-done.2, f32[256,128]{1,0:T(8,128)S(1)} %broadcast_in_dim.22.rcol_ref, ...), custom_call_target="tpu_custom_call" | custom-call | tf_op jit(solution)/shard_map/pallas_call | solution.py:217
  91.2 1.0 copy.15
  92.1 0.0 reduce-scatter.4.cloned.1.call-update
  92.2 0.1 multiply_reduce_fusion
  92.3 34.7 %psum.7 = f32[16]{0:T(128)} all-reduce(f32[16]{0:T(128)S(1)} %multiply_reduce_fusion), channel_id=1, replica_groups=mesh['ctx'=16,'ch'=2] {'ctx'}, use_global_device_ids=true, to_apply=%region_1.2 | all-reduce | flops 16 | bytes 128 | tf_op jit(solution)/shard_map/psum | solution.py:244
  127.0 99.5 %reduce-scatter.4.cloned.1.call-done = f32[16,2]{1,0:T(8,128)} async-done(((f32[512,2]{1,0:T(8,128)}), f32[16,2]{1,0:T(8,128)}) %reduce-scatter.4.cloned.1.call-update) | async-done | bytes 144
  226.5 0.8 fusion
  227.3 0.6 copy.16
  227.9 0.6 copy.17
  228.5 0.7 copy.21
  229.2 0.7 copy.22
  (9 shorter events, 0.1 us)
Async XLA Ops:
  7.2 219.3 %reduce-scatter.4.cloned.1.call-start = ((), (), s32[]{:S(2)}) async-start(), calls=%async_computation.1 | async-start | bytes 270336
  7.2 0.7 copy-start.4
  7.2 0.7 copy-start.5
  77.6 1.2 copy-start
  77.6 1.2 copy-start.1
  78.1 0.7 copy-start.3
  78.8 1.0 copy-start.2
Sparse Core Ops, SparseCore 0:
  92.3 134.1 reduce-scatter.3
where the time goes:
time: 237 us
  blocking collectives  104 us (44%)
  waiting for transfers between devices  99.5 us (42%)
  between operations  14.1 us (6%)
  Pallas kernels  11.3 us (5%)
  local copies, waits for them, and re-layouts  7.15 us (3%)
    unnamed x2, waiting for transfers between devices  99.5 us
    all_gather x1, blocking collectives, shards(): lax.all_gather(jnp.stack([residues, rates]), ('ctx', 'ch'), axis=1, tiled...  69.7 us
    psum x1, blocking collectives, shards(): d_skip = lax.psum(factor * sums[2, :, 0], 'ctx')  34.7 us
    pallas_call x1, Pallas kernels, shards(): pl.pallas_call(functools.partial(body, devs), out_shape=(jax.ShapeDtypeSt...  11.3 us
    unnamed x18, local copies, waits for them, and re-layouts  5.8 us
  transfers between devices with their start and end apart: 1, of which 1 were waited for; matrix products, arithmetic and copies ran while one was open for 0% of the time, Pallas kernels for 0%

commit v1 on v0

--- a/solution.py
+++ b/solution.py
@@ -36,17 +36,65 @@
     return v
 
 
-def body(devs, grad_ref, input_ref, gate_ref, rcol_ref, gcol_ref, rlane_ref, skip_ref,
+def spot(flat, groups):
+    return {"ctx": flat // groups, "ch": lax.rem(flat, groups)}
+
+
+def body(devs, groups, held, factor, grad_ref, input_ref, gate_ref, pack_ref,
          din_ref, dgate_ref, out_ref,
-         xs, gs, p0, p1, g0, g1, ys, zs, wl, send, slots, send_sem, recv_sem):
+         xs, gs, p0, p1, g0, g1, ys, zs, wl, lags, rcols, gcols, tabs, send, slots,
+         row, rows_in, parts_out, parts_in,
+         send_sem, recv_sem, row_send, row_recv, part_send, part_recv):
     seqs, chans, span = grad_ref.shape
     rows = seqs * chans
     count = span // CHUNK
     me = lax.axis_index("ctx")
+    group = lax.axis_index("ch")
+    flat = me * groups + group
+    everyone = devs * groups
+    home = flat // devs
+    place = lax.rem(flat, devs)
+    local = home == group
+    pieces = ORDER // held
     barrier = pltpu.get_barrier_semaphore()
-    for d in range(1, devs):
-        pl.semaphore_signal(barrier, inc=1, device_id={"ctx": lax.rem(me + d, devs)},
+
+    @pl.loop(1, everyone)
+    def _(d):
+        pl.semaphore_signal(barrier, inc=1, device_id=spot(lax.rem(flat + d, everyone), groups),
                             device_id_type=pl.DeviceIdType.MESH)
+
+    def row_copy(e):
+        return pltpu.make_async_remote_copy(
+            src_ref=row.at[0], dst_ref=rows_in.at[place],
+            send_sem=row_send.at[e], recv_sem=row_recv.at[place],
+            device_id={"ctx": e, "ch": home}, device_id_type=pl.DeviceIdType.MESH)
+
+    def row_arrival(e):
+        return pltpu.make_async_remote_copy(
+            src_ref=row.at[0], dst_ref=rows_in.at[e],
+            send_sem=row_send.at[e], recv_sem=row_recv.at[e],
+            device_id={"ctx": e, "ch": home}, device_id_type=pl.DeviceIdType.MESH)
+
+    def part_copy(e):
+        return pltpu.make_async_remote_copy(
+            src_ref=parts_out.at[e // pieces], dst_ref=parts_in.at[me],
+            send_sem=part_send.at[e], recv_sem=part_recv.at[me],
+            device_id=spot(group * devs + e, groups), device_id_type=pl.DeviceIdType.MESH)
+
+    def part_arrival(e):
+        return pltpu.make_async_remote_copy(
+            src_ref=parts_out.at[0], dst_ref=parts_in.at[e],
+            send_sem=part_send.at[e], recv_sem=part_recv.at[e],
+            device_id=spot(group * devs + e, groups), device_id_type=pl.DeviceIdType.MESH)
+
+    def remote(condition, act):
+        pl.when(jnp.logical_not(condition))(act)
+
+    row[0] = pack_ref[chans:chans + 1, :]
+
+    @pl.when(local)
+    def _():
+        rows_in[place] = pack_ref[chans:chans + 1, :]
 
     lane = iota((ORDER, CHUNK), 1).astype(f32)
     rest = jnp.zeros((CHUNK - ORDER, CHUNK), bf16)
@@ -58,11 +106,49 @@
         mid = grad_ref[:, :, at].astype(f32) * gate_ref[:, :, at].astype(f32)
         gs[to, :] = mid.astype(bf16).astype(f32).reshape(rows, CHUNK)
 
+    pl.semaphore_wait(barrier, everyone - 1)
+    for e in range(devs):
+        remote(local & (me == e), lambda e=e: row_copy(e).start())
+
     def pick(c):
         return pl.ds(c, count * seqs, stride=chans)
 
     for c in range(chans):
-        rc = rcol_ref[c * ORDER:(c + 1) * ORDER, :]
+        x = xs[pick(c), :].astype(bf16)
+        g = gs[pick(c), :].astype(bf16)
+        outer = dot(x, g, TN)
+        acc = jnp.zeros((8, CHUNK), f32)
+        for q in range(CHUNK // 8):
+            piece = outer[8 * q:8 * q + 8]
+            keep = iota((8, CHUNK), 1) >= iota((8, CHUNK), 0) + 8 * q
+            acc = acc + turn(jnp.where(keep, piece, 0.0), -8 * q)
+        acc = skew8(acc, -1)
+        lags[8 * c:8 * c + 8, :] = acc
+        wl[2, c:c + 1, :] = jnp.sum(acc, axis=0, keepdims=True)
+
+    for e in range(devs):
+        remote(local & (place == e), lambda e=e: row_arrival(e).wait_recv())
+    for c in range(chans):
+        line = iota((1, CHUNK), 1)
+        res = jnp.zeros((1, CHUNK), f32)
+        rate = jnp.zeros((1, CHUNK), f32)
+        for p in range(pieces):
+            got = rows_in[c * pieces + p]
+            keep = (line >= held * p) & (line < held * (p + 1))
+            res = res + jnp.where(keep, turn(got, held * p), 0.0)
+            rate = rate + jnp.where(keep, turn(got, held * p - held), 0.0)
+        tabs[0, c:c + 1, :] = res
+        tabs[1, c:c + 1, :] = rate
+        own = iota((ORDER, CHUNK), 0) == iota((ORDER, CHUNK), 1)
+        span_of = pl.ds(c * ORDER, ORDER)
+        rcol = jnp.sum(jnp.where(own, jnp.broadcast_to(rate, (ORDER, CHUNK)), 0.0), axis=1, keepdims=True)
+        gain = res * jnp.sqrt(2.0 * rate)
+        gcol = jnp.sum(jnp.where(own, jnp.broadcast_to(gain, (ORDER, CHUNK)), 0.0), axis=1, keepdims=True)
+        rcols[span_of, :] = jnp.broadcast_to(rcol, (ORDER, CHUNK))
+        gcols[span_of, :] = jnp.broadcast_to(gcol, (ORDER, CHUNK))
+
+    for c in range(chans):
+        rc = rcols[c * ORDER:(c + 1) * ORDER, :]
         x = xs[pick(c), :].astype(bf16)
         g = gs[pick(c), :].astype(bf16)
         dec = jnp.exp(-rc * lane)
@@ -77,22 +163,14 @@
         pg = dot(g, wg, NT)
         g0[pick(c), :] = pg[:, :CHUNK]
         g1[pick(c), :] = pg[:, CHUNK:]
-        outer = dot(x, g, TN)
-        acc = jnp.zeros((8, CHUNK), f32)
-        for q in range(CHUNK // 8):
-            piece = outer[8 * q:8 * q + 8]
-            keep = iota((8, CHUNK), 1) >= iota((8, CHUNK), 0) + 8 * q
-            acc = acc + turn(jnp.where(keep, piece, 0.0), -8 * q)
-        acc = skew8(acc, -1)
+        acc = lags[8 * c:8 * c + 8, :]
         high = acc.astype(bf16)
         low = (acc - high.astype(f32)).astype(bf16)
-        local = dot(high, wd, NT) + dot(low, wd, NT)
-        local = jnp.sum(local, axis=0, keepdims=True)
-        wl[0, c:c + 1, :] = local[:, :CHUNK]
-        wl[1, c:c + 1, :] = local[:, CHUNK:]
-        wl[2, c:c + 1, :] = jnp.sum(acc, axis=0, keepdims=True)
-
-    rl = rlane_ref[...]
+        near = jnp.sum(dot(high, wd, NT) + dot(low, wd, NT), axis=0, keepdims=True)
+        wl[0, c:c + 1, :] = near[:, :CHUNK]
+        wl[1, c:c + 1, :] = near[:, CHUNK:]
+
+    rl = jnp.concatenate([tabs[1]] * seqs, 0)
     fade = jnp.exp(-rl * CHUNK)
     zero = jnp.zeros((rows, CHUNK), f32)
     s0, s1, weighted, moment = zero, zero, zero, zero
@@ -120,9 +198,12 @@
         keep = iota((8, CHUNK), 1) < ORDER
         return jnp.concatenate([jnp.where(keep, turn(v, -ORDER * q), 0.0) for q in range(rows // 8)], 0)
 
-    send[0] = pack(s0)
-    send[1] = pack(r0)
-    pl.semaphore_wait(barrier, devs - 1)
+    zeroth = jnp.where(iota((chans, CHUNK), 1) == 0, factor * wl[2], 0.0)
+    skips = jnp.zeros((8, CHUNK), f32)
+    for q in range(chans // 8):
+        skips = skips + turn(zeroth[8 * q:8 * q + 8], ORDER * (rows // 8) + q)
+    send[0] = pack(s0) + skips
+    send[1] = pack(r0) + skips
     copies = []
     for d in range(1, devs):
         copy = pltpu.make_async_remote_copy(
@@ -137,8 +218,8 @@
         copies.append(copy)
 
     for c in range(chans):
-        rc = rcol_ref[c * ORDER:(c + 1) * ORDER, :]
-        gc = gcol_ref[c * ORDER:(c + 1) * ORDER, :]
+        rc = rcols[c * ORDER:(c + 1) * ORDER, :]
+        gc = gcols[c * ORDER:(c + 1) * ORDER, :]
         kern = jnp.sum(gc * jnp.exp(-rc * lane), axis=0, keepdims=True)
         base = skew8(jnp.broadcast_to(kern, (8, CHUNK)), 1)
         parts = []
@@ -148,7 +229,7 @@
         toep = jnp.concatenate(parts, 0).astype(bf16)
         x = xs[pick(c), :]
         g = gs[pick(c), :]
-        sk = skip_ref[c:c + 1, :]
+        sk = pack_ref[c:c + 1, :]
         ys[pick(c), :] = dot(x.astype(bf16), toep, NN) + sk * x
         zs[pick(c), :] = dot(g.astype(bf16), toep, NT) + sk * g
 
@@ -158,6 +239,7 @@
     s_in, sn_in, r_in = (jnp.zeros((8, CHUNK), f32) for _ in range(3))
     for d in range(1, devs):
         v = slots[lax.rem(me + devs - d, devs)]
+        skips = skips + v
         left = jnp.where(me >= d, 1.0, 0.0)
         term = left * jnp.exp(-rp * (span * (d - 1.0))) * v
         s_in = s_in + term
@@ -169,7 +251,20 @@
     for s in range(seqs):
         wl[0] = wl[0] + weighted[s * chans:(s + 1) * chans]
         wl[1] = wl[1] + moment[s * chans:(s + 1) * chans]
-    out_ref[...] = wl[...]
+    res, rate = tabs[0], tabs[1]
+    scale = factor * jnp.sqrt(2.0 * rate)
+    d_res = jnp.where(iota((chans, CHUNK), 1) < ORDER, scale * wl[0], 0.0)
+    d_log = scale * res * (0.5 * wl[0] - rate * wl[1])
+    both = d_res + turn(jnp.where(iota((chans, CHUNK), 1) < ORDER, d_log, 0.0), ORDER)
+    for c in range(chans):
+        parts_out[c] = both[c:c + 1, :]
+    for e in range(devs):
+        remote(local & (place == e), lambda e=e: part_copy(e).start())
+
+        @pl.when(local & (place == e))
+        def _(e=e):
+            parts_in[me] = both[e // pieces:e // pieces + 1, :]
+
 
     for k in range(count):
         to = pl.ds(k * rows, rows)
@@ -181,8 +276,8 @@
         r_in = r_in * fade
 
     for c in range(chans):
-        rc = rcol_ref[c * ORDER:(c + 1) * ORDER, :]
-        gc = gcol_ref[c * ORDER:(c + 1) * ORDER, :]
+        rc = rcols[c * ORDER:(c + 1) * ORDER, :]
+        gc = gcols[c * ORDER:(c + 1) * ORDER, :]
         we = jnp.concatenate([(gc * jnp.exp(-rc * (lane + 1.0))).astype(bf16), rest], 0)
         wp = jnp.concatenate([(gc * jnp.exp(-rc * (CHUNK - 1.0 - lane))).astype(bf16), rest], 0)
         ys[pick(c), :] = ys[pick(c), :] + dot(p0[pick(c), :].astype(bf16), we, NN)
@@ -195,54 +290,64 @@
         dgate_ref[:, :, at] = (grad_ref[:, :, at].astype(f32) * conv).astype(bf16)
         din_ref[:, :, at] = zs[to, :].astype(bf16).reshape(seqs, chans, CHUNK)
 
+    for e in range(devs):
+        remote(local & (me == e), lambda e=e: part_arrival(e).wait_recv())
+    total = parts_in[0]
+    for e in range(1, devs):
+        total = total + parts_in[e]
+    for e in range(devs):
+        remote(local & (me == e), lambda e=e: row_copy(e).wait_send())
+        remote(local & (place == e), lambda e=e: part_copy(e).wait_send())
+    mine = total
+    for p in range(1, pieces):
+        mine = jnp.where(lax.rem(place, pieces) == p, turn(total, -held * p), mine)
+    out_ref[0:8, :] = skips
+    out_ref[8:16, :] = jnp.broadcast_to(mine, (8, CHUNK))
+
 
 def shards(grad_out, inputs, gates, residues, rates, skip):
     seqs, chans, span = grad_out.shape
     devs = lax.axis_size("ctx")
-    group = lax.axis_index("ch")
-    tables = lax.all_gather(jnp.stack([residues, rates]), ("ctx", "ch"), axis=1, tiled=True)
-    total = tables.shape[1] // ORDER
-    tables = tables.reshape(2, total, ORDER)
-    own = lax.dynamic_slice_in_dim(tables, group * chans, chans, axis=1)
-    res, rate = own[0], own[1]
-    amp = jnp.sqrt(2.0 * rate)
-    wide = (chans * ORDER, CHUNK)
-    rcol = jnp.broadcast_to(rate.reshape(-1, 1), wide)
-    gcol = jnp.broadcast_to((res * amp).reshape(-1, 1), wide)
-    rlane = jnp.pad(jnp.tile(rate, (seqs, 1)), ((0, 0), (0, CHUNK - ORDER)))
-    skips = jnp.broadcast_to(skip[:, None], (chans, CHUNK))
-    elems = span // CHUNK * seqs * chans
-    big = pltpu.VMEM((elems, CHUNK), f32)
+    groups = lax.axis_size("ch")
+    held = residues.shape[0]
+    factor = (seqs * span * devs) ** (-0.5)
+    params = jnp.pad(jnp.concatenate([residues, rates]), (0, CHUNK - 2 * held))
+    packed = jnp.concatenate(
+        [jnp.broadcast_to(skip[:, None], (chans, CHUNK)), jnp.broadcast_to(params[None], (8, CHUNK))], 0)
+    big = pltpu.VMEM((span // CHUNK * seqs * chans, CHUNK), f32)
+    line = pltpu.VMEM((chans, 1, CHUNK), f32)
+    lines = pltpu.VMEM((devs, 1, CHUNK), f32)
+    wide = pltpu.VMEM((chans * ORDER, CHUNK), f32)
     vmem = pl.BlockSpec(memory_space=pltpu.VMEM)
     d_input, d_gate, sums = pl.pallas_call(
-        functools.partial(body, devs),
+        functools.partial(body, devs, groups, held, factor),
         out_shape=(
             jax.ShapeDtypeStruct(grad_out.shape, bf16),
             jax.ShapeDtypeStruct(grad_out.shape, bf16),
-            jax.ShapeDtypeStruct((3, chans, CHUNK), f32),
+            jax.ShapeDtypeStruct((16, CHUNK), f32),
         ),
-        in_specs=[vmem] * 7,
+        in_specs=[vmem] * 4,
         out_specs=(vmem, vmem, vmem),
         scratch_shapes=[big] * 8 + [
             pltpu.VMEM((3, chans, CHUNK), f32),
+            pltpu.VMEM((8 * chans, CHUNK), f32),
+            wide,
+            wide,
+            pltpu.VMEM((2, chans, CHUNK), f32),
             pltpu.VMEM((2, 8, CHUNK), f32),
             pltpu.VMEM((devs, 8, CHUNK), f32),
-            pltpu.SemaphoreType.DMA((devs,)),
-            pltpu.SemaphoreType.DMA((devs,)),
-        ],
+            pltpu.VMEM((1, 1, CHUNK), f32),
+            lines,
+            line,
+            lines,
+        ] + [pltpu.SemaphoreType.DMA((devs,))] * 6,
         compiler_params=pltpu.CompilerParams(
             collective_id=0, has_side_effects=True, vmem_limit_bytes=40 * 2 ** 20
         ),
-    )(grad_out, inputs, gates, rcol, gcol, rlane, skips)
-    factor = (seqs * span * devs) ** (-0.5)
-    weighted, moment = sums[0, :, :ORDER], sums[1, :, :ORDER]
-    d_res = factor * amp * weighted
-    d_log = factor * res * amp * (0.5 * weighted - rate * moment)
-    spread = jnp.zeros((2, total, ORDER), f32)
-    spread = lax.dynamic_update_slice_in_dim(spread, jnp.stack([d_res, d_log]), group * chans, axis=1)
-    spread = lax.psum_scatter(spread.reshape(2, -1), ("ctx", "ch"), scatter_dimension=1, tiled=True)
-    d_skip = lax.psum(factor * sums[2, :, 0], "ctx")
-    return (d_input, d_gate, spread[0], spread[1], d_skip)
+    )(grad_out, inputs, gates, packed)
+    first = ORDER * (seqs * chans // 8)
+    d_skip = sums[0:8, first:first + chans // 8].T.reshape(-1)
+    return (d_input, d_gate, sums[8, :held], sums[8, ORDER:ORDER + held], d_skip)
 
 
 def solution(mesh):

time: 237 us -> 28.8 us (0.12)
  blocking collectives: 104 us -> 0 us
  waiting for transfers between devices: 99.5 us -> 0 us
  between operations: 14.1 us -> 0.65 us
  Pallas kernels: 11.3 us -> 20.9 us
    unnamed x2 -> x0, waiting for transfers between devices: 99.5 us -> none
    all_gather x1 -> x0, blocking collectives: 69.7 us -> none  [shards(): lax.all_gather(jnp.stack([residues, rates]), ('ctx', 'ch'), axis=1, tiled...]
    psum x1 -> x0, blocking collectives: 34.7 us -> none  [shards(): d_skip = lax.psum(factor * sums[2, :, 0], 'ctx')]
    pallas_call x1, Pallas kernels: 11.3 us -> 20.9 us  [shards(): pl.pallas_call(functools.partial(body, devs, groups, held, factor), out_s...]
    unnamed x18 -> x10, local copies, waits for them, and re-layouts: 5.8 us -> 4.91 us
  transfers between devices with their start and end apart: 1 -> 0, of which waited for: 1 -> 0; matrix products, arithmetic and copies ran while one was open for 0% -> 0% of each run, Pallas kernels for 0% -> 0%
where the time goes in v1:
time: 28.8 us; the launch traced here: 28.6 us
  Pallas kernels  20.9 us (73%)
  local copies, waits for them, and re-layouts  6.24 us (22%)
  other arithmetic  0.82 us (3%)
  between operations  0.65 us (2%)
    pallas_call x1, Pallas kernels, shards(): pl.pallas_call(functools.partial(body, devs, groups, held, factor), out_s...  20.9 us
    unnamed x10, local copies, waits for them, and re-layouts  4.91 us
    concatenate x1, other arithmetic, shards(): params = jnp.pad(jnp.concatenate([residues, rates]), (0, CHUNK - 2 * held))  0.75 us
    reshape x1, local copies, waits for them, and re-layouts, shards(): d_skip = sums[0:8, first:first + chans // 8].T.reshape(-1)  0.59 us
    squeeze x1, local copies, waits for them, and re-layouts, shards(): sums[8, ORDER:ORDER + held]  0.58 us

profile of v1, /device:TPU:0, one launch (start us, length us, event | category | flops | bytes accessed | tf_op | source)
XLA Modules:
  0.0 28.6 jit_solution(8867149308812296578)
XLA Ops:
  0.6 0.7 %fusion = f32[128]{0:T(128)S(1)} fusion(f32[16]{0:T(128)} %param.10, f32[16]{0:T(128)} %param.9), kind=kLoop, calls=%fused_computation.4 | loop fusion | flops 512 | bytes 640 | tf_op jit(solution)/shard_map/concatenate | solution.py:314
  1.4 0.0 copy-start.3
  1.4 0.7 %copy-done.3 = f32[16]{0:T(128)S(1)} copy-done((f32[16]{0:T(128)S(1)}, f32[16]{0:T(128)}, u32[]{:S(2)}) %copy-start.3) | copy-done | bytes 88
  2.0 0.1 pad_maximum_fusion.pack_ref
  2.1 0.0 copy-start
  2.1 0.9 %copy-done = bf16[2,16,4096]{2,1,0:T(8,128)(2,1)S(1)} copy-done((bf16[2,16,4096]{2,1,0:T(8,128)(2,1)S(1)}, bf16[2,16,4096]{2,1,0:T(8,128)(2,1)}, u32[]{:S(2)}) %copy-start) | copy-done | bytes 262168
  3.1 0.0 copy-start.1
  3.1 0.9 %copy-done.1 = bf16[2,16,4096]{2,1,0:T(8,128)(2,1)S(1)} copy-done((bf16[2,16,4096]{2,1,0:T(8,128)(2,1)S(1)}, bf16[2,16,4096]{2,1,0:T(8,128)(2,1)}, u32[]{:S(2)}) %copy-start.1) | copy-done | bytes 262168
  4.0 0.0 copy-start.2
  4.0 0.9 %copy-done.2 = bf16[2,16,4096]{2,1,0:T(8,128)(2,1)S(1)} copy-done((bf16[2,16,4096]{2,1,0:T(8,128)(2,1)S(1)}, bf16[2,16,4096]{2,1,0:T(8,128)(2,1)}, u32[]{:S(2)}) %copy-start.2) | copy-done | bytes 262168
  5.0 20.9 %shard_map.101 = (bf16[2,16,4096]{2,1,0:T(8,128)(2,1)S(1)}, bf16[2,16,4096]{2,1,0:T(8,128)(2,1)S(1)}, f32[16,128]{1,0:T(8,128)S(1)}) custom-call(bf16[2,16,4096]{2,1,0:T(8,128)(2,1)S(1)} %copy-done, bf16[2,16,4096]{2,1,0:T(8,128)(2,1)S(1)} %copy-done.1, bf16[2,16,4096]{2,1,0:T(8,128)(2,1)S(1)} %copy-done.2, f32[24,128]{1,0:T(8,128)S(1)} %pad_maximum_fusion.pack_ref), custom_call_target="tpu_custom_call" | custom-call | tf_op jit(solution)/shard_map/pallas_call | solution.py:322
  25.9 0.6 %slice_bitcast_fusion.1 = (f32[16]{0:T(128)}, f32[16]{0:T(128)}) fusion(f32[16,128]{1,0:T(8,128)S(1)} %get-tuple-element.10), kind=kLoop, calls=%fused_computation.5 | loop fusion | bytes 256 | tf_op jit(solution)/shard_map/squeeze | solution.py:350
  26.4 0.1 slice_bitcast_fusion
  26.5 0.1 copy.11
  26.6 0.6 %reshape.15 = f32[16]{0:T(128)} reshape(f32[2,8]{1,0:T(2,128)S(1)} %copy.11) | data formatting | bytes 128 | tf_op jit(solution)/shard_map/reshape | solution.py:349
  27.2 0.7 %copy.14 = bf16[2,16,4096]{2,1,0:T(8,128)(2,1)} copy(bf16[2,16,4096]{2,1,0:T(8,128)(2,1)S(1)} %get-tuple-element.18) | data formatting | bytes 524288
  27.9 0.7 %copy.15 = bf16[2,16,4096]{2,1,0:T(8,128)(2,1)} copy(bf16[2,16,4096]{2,1,0:T(8,128)(2,1)S(1)} %get-tuple-element.19) | data formatting | bytes 524288
  (2 shorter events, 0.0 us)
Async XLA Ops:
  1.4 0.7 %copy-start.3 = (f32[16]{0:T(128)S(1)}, f32[16]{0:T(128)}, u32[]{:S(2)}) copy-start(f32[16]{0:T(128)} %param.11) | copy-start | bytes 196
  2.1 1.0 %copy-start = (bf16[2,16,4096]{2,1,0:T(8,128)(2,1)S(1)}, bf16[2,16,4096]{2,1,0:T(8,128)(2,1)}, u32[]{:S(2)}) copy-start(bf16[2,16,4096]{2,1,0:T(8,128)(2,1)} %grad_ref.1) | copy-start | bytes 786436
  3.1 0.9 %copy-start.1 = (bf16[2,16,4096]{2,1,0:T(8,128)(2,1)S(1)}, bf16[2,16,4096]{2,1,0:T(8,128)(2,1)}, u32[]{:S(2)}) copy-start(bf16[2,16,4096]{2,1,0:T(8,128)(2,1)} %input_ref.1) | copy-start | bytes 786436
  4.0 0.9 %copy-start.2 = (bf16[2,16,4096]{2,1,0:T(8,128)(2,1)S(1)}, bf16[2,16,4096]{2,1,0:T(8,128)(2,1)}, u32[]{:S(2)}) copy-start(bf16[2,16,4096]{2,1,0:T(8,128)(2,1)} %gate_ref.1) | copy-start | bytes 786436

commit v2 on v1

--- a/solution.py
+++ b/solution.py
@@ -40,11 +40,17 @@
     return {"ctx": flat // groups, "ch": lax.rem(flat, groups)}
 
 
-def body(devs, groups, held, factor, grad_ref, input_ref, gate_ref, pack_ref,
+def body(devs, groups, held, factor, grad_hbm, input_hbm, gate_hbm, res_hbm, rate_hbm, skip_hbm,
          din_ref, dgate_ref, out_ref,
          xs, gs, p0, p1, g0, g1, ys, zs, wl, lags, rcols, gcols, tabs, send, slots,
          row, rows_in, parts_out, parts_in,
+         grad_ref, input_ref, gate_ref, res_ref, rate_ref, skip_ref, gains, in_sem,
          send_sem, recv_sem, row_send, row_recv, part_send, part_recv):
+    loads = [pltpu.make_async_copy(a, b, in_sem.at[q]) for q, (a, b) in enumerate((
+        (res_hbm, res_ref), (rate_hbm, rate_ref), (skip_hbm, skip_ref),
+        (grad_hbm, grad_ref), (gate_hbm, gate_ref), (input_hbm, input_ref)))]
+    for load in loads:
+        load.start()
     seqs, chans, span = grad_ref.shape
     rows = seqs * chans
     count = span // CHUNK
@@ -90,11 +96,25 @@
     def remote(condition, act):
         pl.when(jnp.logical_not(condition))(act)
 
-    row[0] = pack_ref[chans:chans + 1, :]
+    for load in loads[:3]:
+        load.wait()
+    packed = jnp.concatenate(
+        [res_ref[...], rate_ref[...], jnp.zeros((1, CHUNK - 2 * held), f32)], axis=1)
+    row[0] = packed
 
     @pl.when(local)
     def _():
-        rows_in[place] = pack_ref[chans:chans + 1, :]
+        rows_in[place] = packed
+
+    pl.semaphore_wait(barrier, everyone - 1)
+    for e in range(devs):
+        remote(local & (me == e), lambda e=e: row_copy(e).start())
+    padded = jnp.concatenate([skip_ref[...], jnp.zeros((1, CHUNK - chans), f32)], axis=1)
+    diagonal = iota((chans, CHUNK), 0) == iota((chans, CHUNK), 1)
+    gains[...] = jnp.broadcast_to(jnp.sum(
+        jnp.where(diagonal, jnp.broadcast_to(padded, (chans, CHUNK)), 0.0), axis=1, keepdims=True), (chans, CHUNK))
+    for load in loads[3:]:
+        load.wait()
 
     lane = iota((ORDER, CHUNK), 1).astype(f32)
     rest = jnp.zeros((CHUNK - ORDER, CHUNK), bf16)
@@ -105,10 +125,6 @@
         xs[to, :] = input_ref[:, :, at].astype(f32).reshape(rows, CHUNK)
         mid = grad_ref[:, :, at].astype(f32) * gate_ref[:, :, at].astype(f32)
         gs[to, :] = mid.astype(bf16).astype(f32).reshape(rows, CHUNK)
-
-    pl.semaphore_wait(barrier, everyone - 1)
-    for e in range(devs):
-        remote(local & (me == e), lambda e=e: row_copy(e).start())
 
     def pick(c):
         return pl.ds(c, count * seqs, stride=chans)
@@ -229,7 +245,7 @@
         toep = jnp.concatenate(parts, 0).astype(bf16)
         x = xs[pick(c), :]
         g = gs[pick(c), :]
-        sk = pack_ref[c:c + 1, :]
+        sk = gains[c:c + 1, :]
         ys[pick(c), :] = dot(x.astype(bf16), toep, NN) + sk * x
         zs[pick(c), :] = dot(g.astype(bf16), toep, NT) + sk * g
 
@@ -301,7 +317,12 @@
     mine = total
     for p in range(1, pieces):
         mine = jnp.where(lax.rem(place, pieces) == p, turn(total, -held * p), mine)
-    out_ref[0:8, :] = skips
+    first = ORDER * (rows // 8)
+    spread = jnp.zeros((8, CHUNK), f32)
+    for q in range(chans // 8):
+        column = jnp.sum(jnp.where(iota((8, CHUNK), 1) == first + q, skips, 0.0), axis=1, keepdims=True)
+        spread = spread + jnp.where(iota((8, CHUNK), 1) == iota((8, CHUNK), 0) + 8 * q, column, 0.0)
+    out_ref[0:8, :] = jnp.broadcast_to(jnp.sum(spread, axis=0, keepdims=True), (8, CHUNK))
     out_ref[8:16, :] = jnp.broadcast_to(mine, (8, CHUNK))
 
 
@@ -311,9 +332,6 @@
     groups = lax.axis_size("ch")
     held = residues.shape[0]
     factor = (seqs * span * devs) ** (-0.5)
-    params = jnp.pad(jnp.concatenate([residues, rates]), (0, CHUNK - 2 * held))
-    packed = jnp.concatenate(
-        [jnp.broadcast_to(skip[:, None], (chans, CHUNK)), jnp.broadcast_to(params[None], (8, CHUNK))], 0)
     big = pltpu.VMEM((span // CHUNK * seqs * chans, CHUNK), f32)
     line = pltpu.VMEM((chans, 1, CHUNK), f32)
     lines = pltpu.VMEM((devs, 1, CHUNK), f32)
@@ -326,7 +344,7 @@
             jax.ShapeDtypeStruct(grad_out.shape, bf16),
             jax.ShapeDtypeStruct((16, CHUNK), f32),
         ),
-        in_specs=[vmem] * 4,
+        in_specs=[pl.BlockSpec(memory_space=pltpu.HBM)] * 6,
         out_specs=(vmem, vmem, vmem),
         scratch_shapes=[big] * 8 + [
             pltpu.VMEM((3, chans, CHUNK), f32),
@@ -340,14 +358,20 @@
             lines,
             line,
             lines,
+            pltpu.VMEM(grad_out.shape, bf16),
+            pltpu.VMEM(grad_out.shape, bf16),
+            pltpu.VMEM(grad_out.shape, bf16),
+            pltpu.VMEM((1, held), f32),
+            pltpu.VMEM((1, held), f32),
+            pltpu.VMEM((1, chans), f32),
+            pltpu.VMEM((chans, CHUNK), f32),
+            pltpu.SemaphoreType.DMA((6,)),
         ] + [pltpu.SemaphoreType.DMA((devs,))] * 6,
         compiler_params=pltpu.CompilerParams(
             collective_id=0, has_side_effects=True, vmem_limit_bytes=40 * 2 ** 20
         ),
-    )(grad_out, inputs, gates, packed)
-    first = ORDER * (seqs * chans // 8)
-    d_skip = sums[0:8, first:first + chans // 8].T.reshape(-1)
-    return (d_input, d_gate, sums[8, :held], sums[8, ORDER:ORDER + held], d_skip)
+    )(grad_out, inputs, gates, residues.reshape(1, -1), rates.reshape(1, -1), skip.reshape(1, -1))
+    return (d_input, d_gate, sums[8, :held], sums[8, ORDER:ORDER + held], sums[0, :chans])
 
 
 def solution(mesh):

time: 28.8 us -> 27.6 us (0.958)
  other arithmetic: 0.82 us -> 0 us
  local copies, waits for them, and re-layouts: 6.24 us -> 5.5 us
  Pallas kernels: 20.9 us -> 21.3 us
    concatenate x2 -> x0, other arithmetic: 0.82 us -> none  [the longest x1 0.75 us: shards(): params = jnp.pad(jnp.concatenate([residues, rates]), (0, CHUNK - 2 * held))]
    reshape x1 -> x0, local copies, waits for them, and re-layouts: 0.59 us -> none  [shards(): d_skip = sums[0:8, first:first + chans // 8].T.reshape(-1)]
    pallas_call x1, Pallas kernels: 20.9 us -> 21.3 us  [shards(): pl.pallas_call(functools.partial(body, devs, groups, held, factor), out_s...]
    unnamed x10 -> x14, local copies, waits for them, and re-layouts: 4.91 us -> 4.92 us
where the time goes in v2:
time: 27.6 us; the launch traced here: 27.4 us
  Pallas kernels  21.3 us (77%)
  local copies, waits for them, and re-layouts  5.5 us (20%)
  between operations  0.67 us (2%)
    pallas_call x1, Pallas kernels, shards(): pl.pallas_call(functools.partial(body, devs, groups, held, factor), out_s...  21.3 us
    unnamed x14, local copies, waits for them, and re-layouts  4.92 us
    squeeze x1, local copies, waits for them, and re-layouts, shards(): sums[0, :chans]  0.59 us

profile of v2, /device:TPU:0, one launch (start us, length us, event | category | flops | bytes accessed | tf_op | source)
XLA Modules:
  0.0 27.4 jit_solution(13007223455149860814)
XLA Ops:
  0.6 0.0 copy-start.3
  0.6 0.0 copy-start.4
  0.7 0.0 copy-start.5
  0.7 0.6 %copy-done.3 = f32[16]{0:T(128)S(1)} copy-done((f32[16]{0:T(128)S(1)}, f32[16]{0:T(128)}, u32[]{:S(2)}) %copy-start.3) | copy-done | bytes 88
  1.3 0.0 copy-done.4
  1.3 0.0 copy-done.5
  1.3 0.0 copy-start
  1.3 0.9 %copy-done = bf16[2,16,4096]{2,1,0:T(8,128)(2,1)S(1)} copy-done((bf16[2,16,4096]{2,1,0:T(8,128)(2,1)S(1)}, bf16[2,16,4096]{2,1,0:T(8,128)(2,1)}, u32[]{:S(2)}) %copy-start) | copy-done | bytes 262168
  2.3 0.0 copy-start.1
  2.3 0.9 %copy-done.1 = bf16[2,16,4096]{2,1,0:T(8,128)(2,1)S(1)} copy-done((bf16[2,16,4096]{2,1,0:T(8,128)(2,1)S(1)}, bf16[2,16,4096]{2,1,0:T(8,128)(2,1)}, u32[]{:S(2)}) %copy-start.1) | copy-done | bytes 262168
  3.2 0.0 copy-start.2
  3.2 0.9 %copy-done.2 = bf16[2,16,4096]{2,1,0:T(8,128)(2,1)S(1)} copy-done((bf16[2,16,4096]{2,1,0:T(8,128)(2,1)S(1)}, bf16[2,16,4096]{2,1,0:T(8,128)(2,1)}, u32[]{:S(2)}) %copy-start.2) | copy-done | bytes 262168
  4.2 21.3 %shard_map.101 = (bf16[2,16,4096]{2,1,0:T(8,128)(2,1)S(1)}, bf16[2,16,4096]{2,1,0:T(8,128)(2,1)S(1)}, f32[16,128]{1,0:T(8,128)S(1)}) custom-call(bf16[2,16,4096]{2,1,0:T(8,128)(2,1)S(1)} %copy-done, bf16[2,16,4096]{2,1,0:T(8,128)(2,1)S(1)} %copy-done.1, bf16[2,16,4096]{2,1,0:T(8,128)(2,1)S(1)} %copy-done.2, f32[1,16]{1,0:T(1,128)S(1)} %bitcast.9, ...), custom_call_target="tpu_custom_call" | custom-call | tf_op jit(solution)/shard_map/pallas_call | solution.py:340
  25.4 0.6 %slice_bitcast_fusion = (f32[16]{0:T(128)}, f32[16]{0:T(128)}, f32[16]{0:T(128)}) fusion(f32[16,128]{1,0:T(8,128)S(1)} %get-tuple-element.10), kind=kLoop, calls=%fused_computation | loop fusion | bytes 384 | tf_op jit(solution)/shard_map/squeeze | solution.py:374
  26.0 0.7 %copy.13 = bf16[2,16,4096]{2,1,0:T(8,128)(2,1)} copy(bf16[2,16,4096]{2,1,0:T(8,128)(2,1)S(1)} %get-tuple-element.19) | data formatting | bytes 524288
  26.7 0.7 %copy.14 = bf16[2,16,4096]{2,1,0:T(8,128)(2,1)} copy(bf16[2,16,4096]{2,1,0:T(8,128)(2,1)S(1)} %get-tuple-element.20) | data formatting | bytes 524288
Async XLA Ops:
  0.6 0.7 %copy-start.3 = (f32[16]{0:T(128)S(1)}, f32[16]{0:T(128)}, u32[]{:S(2)}) copy-start(f32[16]{0:T(128)} %param.9) | copy-start | bytes 196
  0.6 0.7 %copy-start.4 = (f32[16]{0:T(128)S(1)}, f32[16]{0:T(128)}, u32[]{:S(2)}) copy-start(f32[16]{0:T(128)} %param.10) | copy-start | bytes 196
  0.7 0.7 %copy-start.5 = (f32[16]{0:T(128)S(1)}, f32[16]{0:T(128)}, u32[]{:S(2)}) copy-start(f32[16]{0:T(128)} %param.11) | copy-start | bytes 196
  1.3 0.9 %copy-start = (bf16[2,16,4096]{2,1,0:T(8,128)(2,1)S(1)}, bf16[2,16,4096]{2,1,0:T(8,128)(2,1)}, u32[]{:S(2)}) copy-start(bf16[2,16,4096]{2,1,0:T(8,128)(2,1)} %grad_hbm.1) | copy-start | bytes 786436
  2.3 0.9 %copy-start.1 = (bf16[2,16,4096]{2,1,0:T(8,128)(2,1)S(1)}, bf16[2,16,4096]{2,1,0:T(8,128)(2,1)}, u32[]{:S(2)}) copy-start(bf16[2,16,4096]{2,1,0:T(8,128)(2,1)} %input_hbm.1) | copy-start | bytes 786436
  3.2 0.9 %copy-start.2 = (bf16[2,16,4096]{2,1,0:T(8,128)(2,1)S(1)}, bf16[2,16,4096]{2,1,0:T(8,128)(2,1)}, u32[]{:S(2)}) copy-start(bf16[2,16,4096]{2,1,0:T(8,128)(2,1)} %gate_hbm.1) | copy-start | bytes 786436

commit v3 on v2

--- a/solution.py
+++ b/solution.py
@@ -368,7 +368,7 @@
             pltpu.SemaphoreType.DMA((6,)),
         ] + [pltpu.SemaphoreType.DMA((devs,))] * 6,
         compiler_params=pltpu.CompilerParams(
-            collective_id=0, has_side_effects=True, vmem_limit_bytes=40 * 2 ** 20
+            collective_id=0, has_side_effects=True, vmem_limit_bytes=67108864
         ),
     )(grad_out, inputs, gates, residues.reshape(1, -1), rates.reshape(1, -1), skip.reshape(1, -1))
     return (d_input, d_gate, sums[8, :held], sums[8, ORDER:ORDER + held], sums[0, :chans])

time: 27.6 us -> 26.5 us (0.960)
  local copies, waits for them, and re-layouts: 5.5 us -> 3.76 us
  Pallas kernels: 21.3 us -> 21.9 us
    unnamed x14 -> x4, local copies, waits for them, and re-layouts: 4.92 us -> 2.42 us
    squeeze x1, local copies, waits for them, and re-layouts: 0.59 us -> 1.34 us  [shards(): sums[0, :chans]]
    pallas_call x1, Pallas kernels: 21.3 us -> 21.9 us  [shards(): pl.pallas_call(functools.partial(body, devs, groups, held, factor), out_s...]
where the time goes in v3:
time: 26.5 us; the launch traced here: 26.3 us
  Pallas kernels  21.9 us (83%)
  local copies, waits for them, and re-layouts  3.76 us (14%)
  between operations  0.64 us (2%)
    pallas_call x1, Pallas kernels, shards(): pl.pallas_call(functools.partial(body, devs, groups, held, factor), out_s...  21.9 us
    unnamed x4, local copies, waits for them, and re-layouts  2.42 us
    squeeze x1, local copies, waits for them, and re-layouts, shards(): sums[0, :chans]  1.34 us

profile of v3, /device:TPU:0, one launch (start us, length us, event | category | flops | bytes accessed | tf_op | source)
XLA Modules:
  0.0 26.3 jit_solution(7678345859663058234)
XLA Ops:
  0.6 21.9 %shard_map.101 = (bf16[2,16,4096]{2,1,0:T(8,128)(2,1)}, bf16[2,16,4096]{2,1,0:T(8,128)(2,1)}, f32[16,128]{1,0:T(8,128)}) custom-call(bf16[2,16,4096]{2,1,0:T(8,128)(2,1)} %grad_hbm.1, bf16[2,16,4096]{2,1,0:T(8,128)(2,1)} %input_hbm.1, bf16[2,16,4096]{2,1,0:T(8,128)(2,1)} %gate_hbm.1, f32[1,16]{1,0:T(1,128)} %bitcast.9, f32[1,16]{1,0:T(1,128)} %bitcast.10, ...), custom_call_target="tpu_custom_call" | custom-call | tf_op jit(solution)/shard_map/pallas_call | solution.py:340
  22.6 1.3 %slice_bitcast_fusion = (f32[16]{0:T(128)}, f32[16]{0:T(128)}, f32[16]{0:T(128)}) fusion(f32[16,128]{1,0:T(8,128)} %get-tuple-element.10), kind=kLoop, calls=%fused_computation | loop fusion | bytes 384 | tf_op jit(solution)/shard_map/squeeze | solution.py:374
  23.9 0.0 copy-start
  23.9 1.7 %copy.13 = bf16[2,16,4096]{2,1,0:T(8,128)(2,1)} copy(bf16[2,16,4096]{2,1,0:T(8,128)(2,1)} %get-tuple-element.19) | data formatting | bytes 524288
  25.6 0.0 copy-done
  25.6 0.7 %copy.14 = bf16[2,16,4096]{2,1,0:T(8,128)(2,1)} copy(bf16[2,16,4096]{2,1,0:T(8,128)(2,1)S(1)} %copy-done) | data formatting | bytes 524288
Async XLA Ops:
  23.9 1.7 %copy-start = (bf16[2,16,4096]{2,1,0:T(8,128)(2,1)S(1)}, bf16[2,16,4096]{2,1,0:T(8,128)(2,1)}, u32[]{:S(2)}) copy-start(bf16[2,16,4096]{2,1,0:T(8,128)(2,1)} %get-tuple-element.20) | copy-start | bytes 786436
